TPU v7x, 512 devices: a whole 4x8x8 slice. The times are simulated.
512 devices in a mesh: row: 32 (over z, x), col: 16 (over y, core).
Axes of the slice: x: 4, y: 8, z: 8, core: 2. Of those that a mesh axis runs over, the one named last changes fastest.
Arguments:
- states: float32 [512, 16, 256], P(('row', 'col')), may hold values from -170 to 170
- direction: float32 [512, 16, 256], P(('row', 'col')), may hold values from -170 to 170
- blocks: float32 [32, 16, 16, 256, 256], P('row', 'col'), may hold values from -0.09375 to 0.09375
- counts: int32 [32, 16], P('row', 'col'), may hold values from 4 to 16, as said below
- block_rows: int32 [32, 16, 16], P('row', 'col'), may hold values from 0 to 15, as said below
- block_cols: int32 [32, 16, 16], P('row', 'col'), may hold values from 0 to 31
- rotation: float32 [48, 16], replicated, may hold values from -0.875 to 0.875
Outputs:
- new_states: float32 [512, 16, 256], P(('row', 'col'))
- new_direction: float32 [512, 16, 256], P(('row', 'col'))
- quotient: float32 [16], replicated
Inputs may be any that keep to these rules, and one draw needn't show every extreme that they name: `counts`: slots at or past an owner's count are unused; some owner fills all 16 slots. `block_rows`: several slots of an owner may name the same position.
All inputs are finite; a program needn't handle non-finite values.
Results may differ from a plain program's by a relative error of at most 0.0003.
Values sent between devices are 32-bit elements; how exact they have to be, the bound alone decides.
A program may use at most 64 MiB of HBM per device.

v0:
```python
import jax
import jax.numpy as jnp
from jax import lax
from jax.sharding import PartitionSpec as P

PRECISE = lax.Precision.HIGHEST


def selector(indices, extent, live):
    positions = jnp.arange(extent, dtype=jnp.int32)
    hits = (indices[:, None] == positions[None, :]) & live[:, None]
    return jnp.where(hits, 1.0, 0.0).astype(jnp.float32)


def body(states, direction, blocks, counts, block_rows, block_cols, rotation):
    matrices = blocks[0, 0]
    row_index = block_rows[0, 0]
    col_index = block_cols[0, 0]
    live_count = counts[0, 0]
    slot_total = matrices.shape[0]
    alive = jnp.arange(slot_total, dtype=jnp.int32) < live_count
    piece_count = states.shape[0]
    states_count = states.shape[1]
    block_order = states.shape[2]
    grid_rows = lax.axis_size("row")
    grid_cols = lax.axis_size("col")
    slab_count = piece_count * grid_cols
    row_pick = selector(row_index, slab_count, alive)
    shards = lax.all_gather(states, "row", axis=0, tiled=True)
    column_pick = selector(col_index, shards.shape[0], alive)
    source = jnp.einsum("sp,pkj->skj", column_pick, shards, precision=PRECISE)
    product = jnp.einsum("skj,sij->ski", source, matrices, precision=PRECISE)
    partial_value = jnp.einsum("sr,ski->rki", row_pick, product, precision=PRECISE)
    forward_part = lax.psum_scatter(partial_value, "col", scatter_dimension=0, tiled=True)
    slab_rows = lax.all_gather(states, "col", axis=0, tiled=True)
    source = jnp.einsum("sr,rkj->skj", row_pick, slab_rows, precision=PRECISE)
    backward = jnp.einsum("skj,sji->ski", source, matrices, precision=PRECISE)
    column_pick = selector(col_index, lax.axis_size("row") * piece_count, alive)
    applied = forward_part + lax.psum_scatter(
        jnp.einsum("sc,ski->cki", column_pick, backward, precision=PRECISE),
        "row",
        scatter_dimension=0,
        tiled=True,
    )
    total_rows = piece_count * block_order * grid_rows * grid_cols
    cross, squares = lax.psum(
        (jnp.sum(states * applied, axis=(0, 2)), jnp.sum(states * states, axis=(0, 2))),
        ("row", "col"),
    )
    quotient = cross / squares
    residual = applied - quotient[None, :, None] * states
    subspace = jnp.concatenate([states, residual, direction], axis=1)
    local_gram = jnp.einsum("bit,bjt->ij", subspace, subspace, precision=PRECISE)
    gram_matrix = lax.psum(local_gram, ("row", "col")) / total_rows
    factor = jnp.linalg.cholesky(gram_matrix)
    tail_rows = jnp.concatenate(
        [jnp.zeros((states_count, states_count), jnp.float32), rotation[states_count:]], axis=0
    )
    targets = jnp.concatenate([rotation, tail_rows], axis=1)
    mixing = jax.scipy.linalg.solve_triangular(factor, targets, lower=True, trans=1)
    result = jnp.einsum("im,bit->bmt", mixing, subspace, precision=PRECISE)
    return (result[:, :states_count], result[:, states_count:], quotient)


def solution(mesh):
    return jax.shard_map(
        body,
        mesh=mesh,
        in_specs=(
            P(("row", "col"), None, None),
            P(("row", "col"), None, None),
            P("row", "col", None, None, None),
            P("row", "col"),
            P("row", "col", None),
            P("row", "col", None),
            P(),
        ),
        out_specs=(P(("row", "col"), None, None), P(("row", "col"), None, None), P()),
        check_vma=False,
    )
```

profile of v0, /device:TPU:1, one launch (start us, length us, event | category | flops | bytes accessed | tf_op | source)
XLA Modules:
  0.0 560.1 jit_solution(11018967652563626760)
XLA Ops:
  7.2 0.0 copy-start
  7.2 0.0 copy-start.4
  7.2 0.0 reduce-scatter.3.cloned.1.call-start
  7.9 44.3 %all_gather.6 = f32[32,16,256]{2,1,0:T(8,128)S(1)} all-gather(f32[1,16,256]{2,1,0:T(8,128)} %param.7), channel_id=1, replica_groups=mesh['row'=32,'col'=16] {'row'}, dimensions={0}, use_global_device_ids=true | all-gather | bytes 540672 | tf_op jit(solution)/shard_map/all_gather | solution.py:29
  52.2 1.3 fusion.4
  53.6 5.8 %fusion.2 = f32[16,16,256]{2,1,0:T(8,128)S(1)} fusion(f32[1,1,16,256,256]{4,3,2,1,0:T(8,128)} %param.9, f32[16,16,256]{2,0,1:T(8,128)S(1)} %fusion.4), kind=kOutput, calls=%fused_computation.2 | convolution fusion | flops 201326592 | bytes 4718592 | tf_op jit(solution)/shard_map/skj,sij->ski/dot_general | solution.py:32
  59.4 0.0 copy-start.3
  59.4 0.0 copy-done.4
  59.4 0.5 fusion.11
  59.9 0.9 copy.17
  60.7 0.0 copy-start.2
  60.7 0.0 copy-start.1
  60.7 0.0 reduce-scatter.3.cloned.1.call-update
  60.8 0.0 reduce-scatter.5.cloned.1.call-start
  60.8 0.0 copy-done
  60.8 31.1 %all_gather.7 = f32[16,16,256]{2,1,0:T(8,128)S(1)} all-gather(f32[1,16,256]{2,1,0:T(8,128)S(1)} %copy-done), channel_id=1, replica_groups=mesh['row'=32,'col'=16] {'col'}, dimensions={0}, use_global_device_ids=true | all-gather | bytes 278528 | tf_op jit(solution)/shard_map/all_gather | solution.py:35
  91.9 0.5 fusion.9
  92.4 4.4 fusion
  96.8 0.0 copy-done.3
  96.8 0.7 fusion.6
  97.6 1.1 copy.18
  98.7 0.0 reduce-scatter.5.cloned.1.call-update
  98.7 0.0 copy-done.2
  98.7 0.1 slice.21
  98.8 27.8 %reduce-scatter.3.cloned.1.call-done = f32[1,16,256]{2,1,0:T(8,128)} async-done(((f32[16,16,256]{2,1,0:T(8,128)}), f32[1,16,256]{2,1,0:T(8,128)}) %reduce-scatter.3.cloned.1.call-update) | async-done | bytes 16400 | tf_op jit(solution)/shard_map/reduce_scatter | solution.py:34
  126.6 219.5 %reduce-scatter.5.cloned.1.call-done = f32[1,16,256]{2,1,0:T(8,128)} async-done(((f32[32,16,256]{2,1,0:T(8,128)}), f32[1,16,256]{2,1,0:T(8,128)}) %reduce-scatter.5.cloned.1.call-update) | async-done | bytes 16400 | tf_op jit(solution)/shard_map/reduce_scatter | solution.py:39
  346.1 0.8 multiply_reduce_fusion
  346.9 100.5 %all-reduce.1 = (f32[16]{0:T(128)S(1)}, f32[16]{0:T(128)S(1)}) all-reduce(f32[16]{0:T(128)S(1)} %get-tuple-element.4, f32[16]{0:T(128)S(1)} %get-tuple-element.3), channel_id=1, replica_groups=mesh['row'=32,'col'=16] {'row','col'}, use_global_device_ids=true, to_apply=%region_3.4 | all-reduce | flops 32 | bytes 256 | tf_op jit(solution)/shard_map/psum | solution.py:46
  447.5 0.0 copy-start.5
  447.5 0.1 multiply_subtract_fusion
  447.5 0.0 copy-done.1
  447.5 0.2 fusion.14
  447.7 94.9 %psum.23 = f32[48,48]{0,1:T(8,128)S(1)} all-reduce(f32[48,48]{0,1:T(8,128)S(1)} %fusion.14), channel_id=1, replica_groups=mesh['row'=32,'col'=16] {'row','col'}, use_global_device_ids=true, to_apply=%region_6.7 | all-reduce | flops 2304 | bytes 18432 | tf_op jit(solution)/shard_map/psum | solution.py:54
  542.7 0.1 copy.20
  542.8 4.4 cholesky.16
  547.2 0.6 compare_reduce_fusion
  547.8 0.7 fusion.15
  548.5 3.7 custom-call.7
  552.2 0.2 fusion.16
  552.4 0.2 convolution_bitcast_fusion
  552.7 0.6 fusion.66
  553.3 0.0 copy-done.5
  (5 shorter events, 0.0 us)
Async XLA Ops:
  7.2 53.6 %copy-start = (f32[1,16,256]{2,1,0:T(8,128)S(1)}, f32[1,16,256]{2,1,0:T(8,128)}, u32[]{:S(2)}) copy-start(f32[1,16,256]{2,1,0:T(8,128)} %param.7) | copy-start | bytes 49156
  7.2 52.2 %copy-start.4 = (s32[1,1,16]{2,1,0:T(1,128)S(1)}, s32[1,1,16]{2,1,0:T(1,128)}, u32[]{:S(2)}) copy-start(s32[1,1,16]{2,1,0:T(1,128)} %param.11) | copy-start | bytes 196
  7.2 119.4 %reduce-scatter.3.cloned.1.call-start = ((), (), s32[]{:S(2)}) async-start(), calls=%async_computation.2 | async-start | bytes 278528 | tf_op jit(solution)/shard_map/reduce_scatter | solution.py:34
  59.4 37.5 %copy-start.3 = (s32[1,1,16]{2,1,0:T(1,128)S(1)}, s32[1,1,16]{2,1,0:T(1,128)}, u32[]{:S(2)}) copy-start(s32[1,1,16]{2,1,0:T(1,128)} %param.12) | copy-start | bytes 196
  60.7 38.0 %copy-start.2 = (f32[48,16]{0,1:T(8,128)S(1)}, f32[48,16]{0,1:T(8,128)}, u32[]{:S(2)}) copy-start(f32[48,16]{0,1:T(8,128)} %param.13) | copy-start | bytes 9220
  60.7 386.8 %copy-start.1 = (f32[1,16,256]{2,1,0:T(8,128)S(1)}, f32[1,16,256]{2,1,0:T(8,128)}, u32[]{:S(2)}) copy-start(f32[1,16,256]{2,1,0:T(8,128)} %param.8) | copy-start | bytes 49156
  60.8 285.3 %reduce-scatter.5.cloned.1.call-start = ((), (), s32[]{:S(2)}) async-start(), calls=%async_computation.3 | async-start | bytes 540672 | tf_op jit(solution)/shard_map/reduce_scatter | solution.py:39
  447.5 105.8 %copy-start.5 = (f32[16]{0:T(128)}, f32[16]{0:T(128)S(1)}, u32[]{:S(2)}) copy-start(f32[16]{0:T(128)S(1)} %div.17) | copy-start | bytes 196
Sparse Core Ops, SparseCore 0:
  60.9 65.6 reduce-scatter.2
  131.6 214.4 reduce-scatter.4
where the time goes:
time: 561 us; the launch traced here: 560 us
  blocking collectives  271 us (48%)
  waiting for transfers between devices  247 us (44%)
  between operations  14.8 us (3%)
  matrix products  13.9 us (2%)
  other arithmetic  10.3 us (2%)
    reduce_scatter x1, waiting for transfers between devices, body(): lax.psum_scatter(jnp.einsum('sc,ski->cki', column_pick, backward, precisi...  219 us
    psum x1, blocking collectives, body(): lax.psum((jnp.sum(states * applied, axis=(0, 2)), jnp.sum(states * states...  101 us
    psum x1, blocking collectives, body(): gram_matrix = lax.psum(local_gram, ('row', 'col')) / total_rows  94.9 us
    all_gather x1, blocking collectives, body(): shards = lax.all_gather(states, 'row', axis=0, tiled=True)  44.3 us
    all_gather x1, blocking collectives, body(): slab_rows = lax.all_gather(states, 'col', axis=0, tiled=True)  31.1 us
    reduce_scatter x1, waiting for transfers between devices, body(): lax.psum_scatter(partial_value, 'col', scatter_dimension=0, tiled=True)  27.8 us
  transfers between devices with their start and end apart: 2, of which 2 were waited for; matrix products, arithmetic and copies ran while one was open for 1% of the time, Pallas kernels for 0%

commit v1 on v0

v1 whole, which is shorter than its diff:
```python
import functools

import jax
import jax.numpy as jnp
from jax import lax
from jax.experimental import pallas as pl
from jax.experimental.pallas import tpu as pltpu
from jax.sharding import PartitionSpec as P

MESH = pl.DeviceIdType.MESH
HIGHEST = lax.Precision.HIGHEST
NX, NY, NZ, NC = 4, 8, 8, 2
SLOTS, K, BS, NSUB = 16, 16, 256, 48
F32, BF16 = jnp.float32, jnp.bfloat16

GZ, GX, GY, GC, RX, RZ, RC, RY = range(8)
EARLY, CROSS, LATE = 8, 12, 16
STAGES = 20


def dot(a, b, ca=1, cb=0, precision=HIGHEST):
    return lax.dot_general(a, b, (((ca,), (cb,)), ((), ())), precision=precision, preferred_element_type=F32)


def split(v):
    high = v.astype(BF16)
    return high, (v - high.astype(F32)).astype(BF16)


def inverse_factor(gram, order):
    rows = lax.broadcasted_iota(jnp.int32, (order, 1), 0)
    eye = (
        lax.broadcasted_iota(jnp.int32, (order, order), 0) == lax.broadcasted_iota(jnp.int32, (order, order), 1)
    ).astype(F32)
    work = jnp.concatenate([gram, eye], axis=1)
    for j in range(order - 1):
        pivot_row = work[j : j + 1, :]
        factor = jnp.where(rows > j, work[:, j : j + 1] / work[j : j + 1, j : j + 1], 0.0)
        work = work - factor * pivot_row
    pivots = jnp.sum(work[:, :order] * eye, axis=1, keepdims=True)
    return work[:, order:] / jnp.sqrt(pivots)


def kernel(
    states_hbm, direction_hbm, blocks_hbm, count_hbm, rows_hbm, cols_hbm, rotation_hbm,
    new_states_ref, new_direction_ref, quotient_ref,
    mat, high, low, xr, xc, products, pb, pf, rbx, rbz, rfc, rfy, direction, ar_c, ar_x, ar_y, ar_z,
    count_ref, rows_ref, cols_ref, rotation_ref, load_sem, block_sem, send_sem, recv_sem,
):
    row, col = lax.axis_index("row"), lax.axis_index("col")
    z, x = lax.div(row, NX), lax.rem(row, NX)
    y, core = lax.div(col, NC), lax.rem(col, NC)
    x_peers = [((lax.rem(x + d, NX)), (z * NX + lax.rem(x + d, NX), col)) for d in range(1, NX)]
    z_peers = [((lax.rem(z + d, NZ)), (lax.rem(z + d, NZ) * NX + x, col)) for d in range(1, NZ)]
    y_peers = [((lax.rem(y + d, NY)), (row, lax.rem(y + d, NY) * NC + core)) for d in range(1, NY)]
    c_peers = [(1 - core, (row, y * NC + 1 - core))]

    def load(src, dst, index):
        return pltpu.make_async_copy(src, dst, load_sem.at[index])

    def block_load(s):
        return pltpu.make_async_copy(blocks_hbm.at[0, 0, s], mat.at[s], block_sem.at[s])

    def send(stage, src, dst, device):
        pltpu.make_async_remote_copy(
            src_ref=src, dst_ref=dst, send_sem=send_sem.at[stage], recv_sem=recv_sem.at[stage],
            device_id=device, device_id_type=MESH,
        ).start()

    def arrived(stage, like):
        pltpu.make_async_copy(like, like, recv_sem.at[stage]).wait()

    def sent(stage, like):
        pltpu.make_async_copy(like, like, send_sem.at[stage]).wait()

    loads = [
        load(states_hbm.at[0], xr.at[x, z], 0),
        load(states_hbm.at[0], xc.at[core, y], 1),
        load(direction_hbm.at[0], direction, 2),
        load(count_hbm, count_ref, 3),
        load(rows_hbm, rows_ref, 4),
        load(cols_hbm, cols_ref, 5),
        load(rotation_hbm, rotation_ref, 6),
    ]
    for copy in loads:
        copy.start()
    for s in range(SLOTS):
        block_load(s).start()

    barrier = pltpu.get_barrier_semaphore()
    peers = [device for _, device in x_peers + z_peers + y_peers + c_peers]
    for device in peers:
        pl.semaphore_signal(barrier, inc=1, device_id=device, device_id_type=MESH)
    pl.semaphore_wait(barrier, len(peers))

    loads[0].wait()
    loads[1].wait()
    for _, device in z_peers:
        send(GZ, xr.at[x, z], xr.at[x, z], device)
    for _, device in y_peers:
        send(GY, xc.at[core, y], xc.at[core, y], device)

    ar_stages = [(ar_c, core, c_peers, NC), (ar_x, x, x_peers, NX), (ar_y, y, y_peers, NY), (ar_z, z, z_peers, NZ)]

    def ar_send(which, stage, value):
        buffer, me, others, _ = ar_stages[stage]
        place = (which - EARLY) // 4
        buffer[place, me] = value
        for _, device in others:
            send(which + stage, buffer.at[place, me], buffer.at[place, me], device)

    def ar_sum(which, stage):
        buffer, _, _, n = ar_stages[stage]
        place = (which - EARLY) // 4
        arrived(which + stage, buffer.at[place, 0 : n - 1])
        total = buffer[place, 0]
        for i in range(1, n):
            total = total + buffer[place, i]
        return total

    def ar_next(which, stage):
        ar_send(which, stage + 1, ar_sum(which, stage))

    states = xr[x, z]
    loads[2].wait()
    directions = direction[...]
    both = jnp.concatenate([states, directions], axis=0)
    gram = dot(both, both, 1, 1)
    ar_send(EARLY, 0, jnp.concatenate([gram[0:8], gram[8:16], gram[16:24], gram[24:32]], axis=1))

    def convert(s, carry):
        block_load(s).wait()
        h, l = split(mat[s])
        high[s] = h
        low[s] = l
        return carry

    lax.fori_loop(0, SLOTS // 2, convert, 0)
    arrived(GY, xc.at[core, 0 : NY - 1])
    send(GC, xc.at[core], xc.at[core], c_peers[0][1])
    ar_next(EARLY, 0)
    arrived(GZ, xr.at[x, 0 : NZ - 1])
    for _, device in x_peers:
        send(GX, xr.at[x], xr.at[x], device)
    lax.fori_loop(SLOTS // 2, SLOTS, convert, 0)
    ar_next(EARLY, 1)

    for copy in loads[3:6]:
        copy.wait()
    live = count_ref[0, 0]

    arrived(GC, xc.at[core])

    def backward(s, carry):
        place = rows_ref[0, 0, s]
        alive = jnp.where(s < live, 1.0, 0.0)
        source = xc[lax.rem(place, NC), lax.div(place, NC)] * alive
        h, l = split(source)
        both = dot(jnp.concatenate([h, l], axis=0), high[s], 1, 0, None)
        products[s] = both[:K] + both[K:] + dot(h, low[s], 1, 0, None)
        return carry

    lax.fori_loop(0, SLOTS, backward, 0)

    def pick(target, wanted, index_ref):
        total = jnp.zeros((K, BS), F32)
        for s in range(SLOTS):
            total = total + jnp.where(index_ref[0, 0, s] == wanted, 1.0, 0.0) * products[s]
        return total

    for index, device in x_peers + [(x, None)]:

        def fill(zz, carry, index=index):
            pb[index, zz] = pick(pb, zz * NX + index, cols_ref)
            return carry

        lax.fori_loop(0, NZ, fill, 0)
        if device is not None:
            send(RX, pb.at[index], rbx.at[x], device)

    ar_next(EARLY, 2)

    arrived(GX, xr.at[0 : NX - 1])

    def crossing(s, total):
        place = cols_ref[0, 0, s]
        return total + products[s] * xr[lax.rem(place, NX), lax.div(place, NX)]

    cross = lax.fori_loop(0, SLOTS, crossing, jnp.zeros((K, BS), F32))
    cross = 2.0 * jnp.sum(cross, axis=1, keepdims=True)
    lanes = lax.broadcasted_iota(jnp.int32, (8, 128), 1)
    ar_send(CROSS, 0, jnp.where(lanes < 64, cross[:8], cross[8:]))

    def forward(s, carry):
        place = cols_ref[0, 0, s]
        alive = jnp.where(s < live, 1.0, 0.0)
        source = xr[lax.rem(place, NX), lax.div(place, NX)] * alive
        h, l = split(source)
        both = dot(jnp.concatenate([h, l], axis=0), high[s], 1, 1, None)
        products[s] = both[:K] + both[K:] + dot(h, low[s], 1, 1, None)
        return carry

    lax.fori_loop(0, SLOTS, forward, 0)
    for index, device in c_peers + [(core, None)]:

        def fill(yy, carry, index=index):
            pf[index, yy] = pick(pf, yy * NC + index, rows_ref)
            return carry

        lax.fori_loop(0, NY, fill, 0)
        if device is not None:
            send(RC, pf.at[index], rfc, device)
    ar_next(CROSS, 0)

    arrived(RX, rbx.at[0 : NX - 1])

    def sum_x(zz, carry):
        total = pb[x, zz]
        for d in range(1, NX):
            total = total + rbx[lax.rem(x + d, NX), zz]
        pb[x, zz] = total
        return carry

    lax.fori_loop(0, NZ, sum_x, 0)
    for index, device in z_peers:
        send(RZ, pb.at[x, index], rbz.at[z], device)

    arrived(RC, rfc)

    def sum_c(yy, carry):
        pf[core, yy] = pf[core, yy] + rfc[yy]
        return carry

    lax.fori_loop(0, NY, sum_c, 0)
    for index, device in y_peers:
        send(RY, pf.at[core, index], rfy.at[y], device)
    ar_next(CROSS, 1)

    total_rows = BS * NZ * NX * NY * NC
    packed = ar_sum(EARLY, 3) / total_rows
    gram = jnp.concatenate([packed[:, 32 * i : 32 * i + 32] for i in range(4)], axis=0)
    squares = jnp.sum(
        jnp.where(
            lax.broadcasted_iota(jnp.int32, (K, K), 0) == lax.broadcasted_iota(jnp.int32, (K, K), 1),
            gram[:K, :K], 0.0,
        ),
        axis=1, keepdims=True,
    )
    inverse = inverse_factor(gram[:K, :K], K)
    basis = dot(inverse, states)
    project = dot(gram[K:, :K], inverse, 1, 1)
    rest = directions - dot(project, basis)
    gram_rest = gram[K:, K:] - dot(project, project, 1, 1)
    loads[6].wait()
    rotation = rotation_ref[...]
    kept = dot(rotation[:, :K], basis)

    ar_next(CROSS, 2)
    arrived(RY, rfy.at[0 : NY - 1])
    applied = pf[core, y]
    for d in range(1, NY):
        applied = applied + rfy[lax.rem(y + d, NY)]
    arrived(RZ, rbz.at[0 : NZ - 1])
    applied = applied + pb[x, z]
    for d in range(1, NZ):
        applied = applied + rbz[lax.rem(z + d, NZ)]
    crossed = ar_sum(CROSS, 3)
    quotient = jnp.concatenate([crossed[:, 0:1], crossed[:, 64:65]], axis=0) / (squares * total_rows)
    residual = applied - quotient * states
    quotient_ref[...] = jnp.sum(
        jnp.where(
            lax.broadcasted_iota(jnp.int32, (K, K), 0) == lax.broadcasted_iota(jnp.int32, (K, K), 1), quotient, 0.0
        ),
        axis=0, keepdims=True,
    )

    left = jnp.concatenate([residual, rest], axis=0)
    right = jnp.concatenate([basis, residual, rest], axis=0)
    local = dot(left, right, 1, 1)
    wide = jnp.concatenate([local[:K], local[K:, K : 2 * K]], axis=1)
    ar_send(LATE, 0, jnp.concatenate([wide[:8], wide[8:]], axis=1))
    ar_next(LATE, 0)
    ar_next(LATE, 1)
    ar_next(LATE, 2)
    packed = ar_sum(LATE, 3) / total_rows
    wide = jnp.concatenate([packed[:, :64], packed[:, 64:]], axis=0)
    lower = wide[:, :K]
    gram_residual = wide[:, K : 2 * K] - dot(lower, lower, 1, 1)
    top = jnp.concatenate([gram_residual, wide[:, 2 * K : 3 * K]], axis=1)
    bottom = jnp.concatenate([wide[:, 3 * K :], gram_rest], axis=1)
    inverse = inverse_factor(jnp.concatenate([top, bottom], axis=0), 2 * K)
    mixing = dot(rotation[:, K:], inverse)
    mixing = jnp.concatenate([-dot(mixing[:, :K], lower), mixing], axis=1)
    fresh = dot(mixing, right)
    new_direction_ref[0] = fresh
    new_states_ref[0] = kept + new_direction_ref[0]

    sent(GZ, xr.at[x, 0 : NZ - 1])
    sent(GX, xr.at[0 : NX - 1])
    sent(GY, xc.at[core, 0 : NY - 1])
    sent(GC, xc.at[core])
    sent(RX, rbx.at[0 : NX - 1])
    sent(RZ, rbz.at[0 : NZ - 1])
    sent(RC, rfc)
    sent(RY, rfy.at[0 : NY - 1])
    for which in (EARLY, CROSS, LATE):
        for stage in range(4):
            buffer, _, _, n = ar_stages[stage]
            sent(which + stage, buffer.at[0, 0 : n - 1])


def body(states, direction, blocks, counts, block_rows, block_cols, rotation):
    vmem = pl.BlockSpec(memory_space=pltpu.VMEM)
    hbm = pl.BlockSpec(memory_space=pl.ANY)
    new_states, new_direction, quotient = pl.pallas_call(
        kernel,
        out_shape=(
            jax.ShapeDtypeStruct((1, K, BS), F32),
            jax.ShapeDtypeStruct((1, K, BS), F32),
            jax.ShapeDtypeStruct((1, K), F32),
        ),
        in_specs=[hbm] * 7,
        out_specs=(vmem, vmem, vmem),
        scratch_shapes=[
            pltpu.VMEM((SLOTS, BS, BS), F32),
            pltpu.VMEM((SLOTS, BS, BS), BF16),
            pltpu.VMEM((SLOTS, BS, BS), BF16),
            pltpu.VMEM((NX, NZ, K, BS), F32),
            pltpu.VMEM((NC, NY, K, BS), F32),
            pltpu.VMEM((SLOTS, K, BS), F32),
            pltpu.VMEM((NX, NZ, K, BS), F32),
            pltpu.VMEM((NC, NY, K, BS), F32),
            pltpu.VMEM((NX, NZ, K, BS), F32),
            pltpu.VMEM((NZ, K, BS), F32),
            pltpu.VMEM((NY, K, BS), F32),
            pltpu.VMEM((NY, K, BS), F32),
            pltpu.VMEM((K, BS), F32),
            pltpu.VMEM((3, NC, 8, 128), F32),
            pltpu.VMEM((3, NX, 8, 128), F32),
            pltpu.VMEM((3, NY, 8, 128), F32),
            pltpu.VMEM((3, NZ, 8, 128), F32),
            pltpu.SMEM((1, 1), jnp.int32),
            pltpu.SMEM((1, 1, SLOTS), jnp.int32),
            pltpu.SMEM((1, 1, SLOTS), jnp.int32),
            pltpu.VMEM((K, NSUB), F32),
            pltpu.SemaphoreType.DMA((7,)),
            pltpu.SemaphoreType.DMA((SLOTS,)),
            pltpu.SemaphoreType.DMA((STAGES,)),
            pltpu.SemaphoreType.DMA((STAGES,)),
        ],
        compiler_params=pltpu.CompilerParams(
            collective_id=0, has_side_effects=True, vmem_limit_bytes=60 * 1024 * 1024
        ),
    )(states, direction, blocks, counts, block_rows, block_cols, rotation.T)
    return new_states, new_direction, quotient.reshape(K)


def solution(mesh):
    return jax.shard_map(
        body,
        mesh=mesh,
        in_specs=(
            P(("row", "col"), None, None),
            P(("row", "col"), None, None),
            P("row", "col", None, None, None),
            P("row", "col"),
            P("row", "col", None),
            P("row", "col", None),
            P(),
        ),
        out_specs=(P(("row", "col"), None, None), P(("row", "col"), None, None), P()),
        check_vma=False,
    )
```

time: 561 us -> 68.7 us (0.12)
  blocking collectives: 271 us -> 0 us
  waiting for transfers between devices: 247 us -> 0 us
  Pallas kernels: 0 us -> 63.3 us
  matrix products: 13.9 us -> 0 us
  between operations: 14.8 us -> 1.29 us
  other arithmetic: 10.3 us -> 0 us
    reduce_scatter x2 -> x0, waiting for transfers between devices: 247 us -> none  [the longest x1 219 us: body(): lax.psum_scatter(jnp.einsum('sc,ski->cki', column_pick, backward, precisi...]
    psum x2 -> x0, blocking collectives: 195 us -> none  [the longest x1 101 us: body(): lax.psum((jnp.sum(states * applied, axis=(0, 2)), jnp.sum(states * states...]
    all_gather x2 -> x0, blocking collectives: 75.4 us -> none  [the longest x1 44.3 us: body(): shards = lax.all_gather(states, 'row', axis=0, tiled=True)]
    pallas_call x0 -> x1, Pallas kernels: none -> 63.3 us  [body(): pl.pallas_call(kernel, out_shape=(jax.ShapeDtypeStruct((1, K, BS), F32),...]
    dot_general x8 -> x0, matrix products: 13.7 us -> none  [the longest x1 5.81 us: body(): product = jnp.einsum('skj,sij->ski', source, matrices, precision=PRECISE)]
    another operation x5 -> x0, other arithmetic: 9.38 us -> none  [the longest x3 5.05 us: body(): factor = jnp.linalg.cholesky(gram_matrix)]
  transfers between devices with their start and end apart: 2 -> 0, of which waited for: 2 -> 0; matrix products, arithmetic and copies ran while one was open for 1% -> 0% of each run, Pallas kernels for 0% -> 0%
where the time goes in v1:
time: 68.7 us; the launch traced here: 68.4 us
  Pallas kernels  63.3 us (92%)
  local copies, waits for them, and re-layouts  3.82 us (6%)
  between operations  1.29 us (2%)
    pallas_call x1, Pallas kernels, body(): pl.pallas_call(kernel, out_shape=(jax.ShapeDtypeStruct((1, K, BS), F32),...  63.3 us
    unnamed x3, local copies, waits for them, and re-layouts  3.82 us

profile of v1, /device:TPU:1, one launch (start us, length us, event | category | flops | bytes accessed | tf_op | source)
XLA Modules:
  0.0 68.4 jit_solution(16410893213978305498)
XLA Ops:
  1.3 63.3 %shard_map.94 = (f32[1,16,256]{2,1,0:T(8,128)}, f32[1,16,256]{2,1,0:T(8,128)}, f32[1,16]{1,0:T(1,128)}) custom-call(f32[1,16,256]{2,1,0:T(8,128)} %states_hbm.1, f32[1,16,256]{2,1,0:T(8,128)} %direction_hbm.1, f32[1,1,16,256,256]{4,3,2,1,0:T(8,128)} %blocks_hbm.1, s32[1,1]{1,0:T(1,128)S(6)} %copy.13.count_hbm, s32[1,1,16]{2,1,0:T(1,128)} %rows_hbm.1, ...), custom_call_target="tpu_custom_call" | custom-call | tf_op jit(solution)/shard_map/pallas_call | solution.py:315
  64.6 1.3 %copy.14 = f32[1,16,256]{2,1,0:T(8,128)} copy(f32[1,16,256]{2,1,0:T(8,128)} %get-tuple-element.12) | data formatting | bytes 32768
  65.9 1.3 %copy.15 = f32[1,16,256]{2,1,0:T(8,128)} copy(f32[1,16,256]{2,1,0:T(8,128)} %get-tuple-element.13) | data formatting | bytes 32768
  67.2 1.2 %copy.16 = f32[16]{0:T(128)} copy(f32[16]{0:T(128)} %bitcast.3) | data formatting | bytes 128

commit v2 on v1

v2 whole, which is shorter than its diff:
```python
import jax
import jax.numpy as jnp
from jax import lax
from jax.experimental import pallas as pl
from jax.experimental.pallas import tpu as pltpu
from jax.sharding import PartitionSpec as P

MESH = pl.DeviceIdType.MESH
HIGHEST = lax.Precision.HIGHEST
NX, NY, NZ, NC = 4, 8, 8, 2
SLOTS, K, BS, NSUB = 16, 16, 256, 48
F32, BF16 = jnp.float32, jnp.bfloat16
GATHER_GROUPS = ((0, 1), (1, 3), (3, 5), (5, 8))
SCATTER_GROUPS = ((3, 8), (0, 3))
X_ORDER = (2, 1, 3)
STAGES = 64


def place_of(offset):
    return jnp.where(offset <= NZ // 2, jnp.maximum(2 * offset - 1, 0), 2 * (NZ - offset))


def offset_of(place):
    return jnp.where(lax.rem(place, 2) == 1, lax.div(place + 1, 2), lax.rem(NZ - lax.div(place, 2), NZ))


PLACE = [0 if d == 0 else 2 * d - 1 if d <= NZ // 2 else 2 * (NZ - d) for d in range(NZ)]


def dot(a, b, ca=1, cb=0, precision=HIGHEST):
    return lax.dot_general(a, b, (((ca,), (cb,)), ((), ())), precision=precision, preferred_element_type=F32)


def split(v):
    high = v.astype(BF16)
    return high, (v - high.astype(F32)).astype(BF16)


def identity(order):
    return (
        lax.broadcasted_iota(jnp.int32, (order, order), 0) == lax.broadcasted_iota(jnp.int32, (order, order), 1)
    ).astype(F32)


def inverse_factor(gram, order):
    shape = (order, 128)
    rows = lax.broadcasted_iota(jnp.int32, shape, 0)
    eye = identity(order)
    work = jnp.concatenate([gram, eye, jnp.zeros((order, 128 - 2 * order), F32)], axis=1)

    def wide(part):
        return jnp.broadcast_to(part, shape)

    for j in range(0, order, 2):
        u, v = wide(work[:, j : j + 1]), wide(work[:, j + 1 : j + 2])
        first, second = wide(work[j : j + 1, :]), wide(work[j + 1 : j + 2, :])
        a, b, c = wide(u[j : j + 1, :]), wide(v[j : j + 1, :]), wide(v[j + 1 : j + 2, :])
        scale = 1.0 / (a * c - b * b)
        below = u * ((c * first - b * second) * scale) + v * ((a * second - b * first) * scale)
        work = work - jnp.where(rows > j + 1, below, jnp.where(rows == j + 1, (b / a) * first, 0.0))
    pivots = jnp.sum(work[:, :order] * eye, axis=1, keepdims=True)
    return work[:, order : 2 * order] / jnp.sqrt(pivots)


def kernel(
    states_hbm, direction_hbm, blocks_hbm, count_hbm, rows_hbm, cols_hbm, rotation_hbm,
    new_states_ref, new_direction_ref, quotient_ref,
    mat, high, low, xr, xc, products, pb, pf, rbx, rbz, rfc, rfy, direction,
    ar_c, ar_x, ar_y, ar_z, count_ref, rows_ref, cols_ref, rotation_ref, load_sem, block_sem, send_sem, recv_sem,
):
    row, col = lax.axis_index("row"), lax.axis_index("col")
    z, x = lax.div(row, NX), lax.rem(row, NX)
    y, core = lax.div(col, NC), lax.rem(col, NC)
    x_peers = [(z * NX + lax.rem(x + d, NX), col) for d in range(1, NX)]
    z_order = sorted(range(1, NZ), key=lambda d: -min(d, NZ - d))
    z_peers = [(lax.rem(z + d, NZ) * NX + x, col) for d in z_order]
    y_peers = [(lax.rem(y + d, NY), (row, lax.rem(y + d, NY) * NC + core)) for d in sorted(range(1, NY), key=lambda d: -min(d, NY - d))]
    other_core = (row, y * NC + 1 - core)

    stages, drains = {}, []

    def stage_of(name):
        return stages.setdefault(name, len(stages))

    def load(src, dst, index):
        return pltpu.make_async_copy(src, dst, load_sem.at[index])

    def block_load(s):
        return pltpu.make_async_copy(blocks_hbm.at[0, 0, s], mat.at[s], block_sem.at[s])

    def send(name, src, dst, device, recv_name=None):
        pltpu.make_async_remote_copy(
            src_ref=src, dst_ref=dst, send_sem=send_sem.at[stage_of(name)],
            recv_sem=recv_sem.at[stage_of(recv_name or name)], device_id=device, device_id_type=MESH,
        ).start()

    def send_one(name, src, dst, device):
        send(name, src, dst, device)
        drains.append((name, src))

    def arrived(name, like):
        pltpu.make_async_copy(like, like, recv_sem.at[stage_of(name)]).wait()

    loads = [
        load(states_hbm.at[0], xr.at[x, 0], 0),
        load(states_hbm.at[0], xc.at[core, y], 1),
        load(direction_hbm.at[0], direction, 2),
        load(count_hbm, count_ref, 3),
        load(rows_hbm, rows_ref, 4),
        load(cols_hbm, cols_ref, 5),
        load(rotation_hbm, rotation_ref, 6),
    ]
    barrier = pltpu.get_barrier_semaphore()
    peers = z_peers + [device for _, device in y_peers] + x_peers + [other_core]
    for device in peers:
        pl.semaphore_signal(barrier, inc=1, device_id=device, device_id_type=MESH)
    for copy in loads:
        copy.start()
    for s in range(SLOTS):
        block_load(s).start()

    pl.semaphore_wait(barrier, len(peers))

    def gather_group(place):
        return [i for i, (a, b) in enumerate(GATHER_GROUPS) if a <= place < b][0]

    loads[0].wait()
    for d, device in zip(z_order, z_peers):
        there = PLACE[NZ - d]
        send("gz", xr.at[x, 0], xr.at[x, there], device, ("gz", gather_group(there)))
    drains.append(("gz", xr.at[0, 0 : NZ - 1]))
    def gather_x(g):
        a, b = GATHER_GROUPS[g]
        if g > 0:
            arrived(("gz", g), xr.at[x, a:b])
        for d in X_ORDER:
            send_one(("gx", d, g), xr.at[x, a:b], xr.at[x, a:b], x_peers[d - 1])

    ar_stages = [
        (ar_c, core, [other_core], NC), (ar_y, y, [device for _, device in y_peers], NY),
        (ar_z, z, z_peers, NZ), (ar_x, x, x_peers, NX),
    ]
    EARLY, CROSS, LATE = range(3)

    def ar_send(which, stage, value):
        buffer, me, others, n = ar_stages[stage]
        buffer[which, me] = value
        for device in others:
            send(("ar", which, stage), buffer.at[which, me], buffer.at[which, me], device)
        drains.append((("ar", which, stage), buffer.at[which, 0 : n - 1]))

    def ar_sum(which, stage):
        buffer, _, _, n = ar_stages[stage]
        arrived(("ar", which, stage), buffer.at[which, 0 : n - 1])
        total = [buffer[which, i] for i in range(n)]
        while len(total) > 1:
            total = [total[i] + total[i + 1] for i in range(0, len(total), 2)]
        return total[0]

    def ar_next(which, stage):
        ar_send(which, stage + 1, ar_sum(which, stage))

    def convert(s, carry):
        block_load(s).wait()
        h, l = split(mat[s])
        high[s] = h
        low[s] = l
        return carry

    gather_x(0)
    loads[1].wait()
    for _, device in y_peers:
        send("gy", xc.at[core, y], xc.at[core, y], device)
    drains.append(("gy", xc.at[0, 0 : NY - 1]))
    states = xr[x, 0]
    loads[2].wait()
    directions = direction[...]
    both = jnp.concatenate([states, directions], axis=0)
    gram = dot(both, both, 1, 1)
    ar_send(EARLY, 0, jnp.concatenate([gram[0:8], gram[8:16], gram[16:24], gram[24:32]], axis=1))
    for g in range(1, len(GATHER_GROUPS) - 1):
        gather_x(g)
    lax.fori_loop(0, SLOTS, convert, 0)
    gather_x(len(GATHER_GROUPS) - 1)
    arrived("gy", xc.at[0, 0 : NY - 1])
    send_one("gc", xc.at[core], xc.at[core], other_core)
    ar_next(EARLY, 0)
    for copy in loads[3:6]:
        copy.wait()
    live = count_ref[0, 0]

    arrived("gc", xc.at[core])

    def backward(s, carry):
        place = rows_ref[0, 0, s]
        alive = jnp.where(s < live, 1.0, 0.0)
        source = xc[lax.rem(place, NC), lax.div(place, NC)] * alive
        h, l = split(source)
        both = dot(jnp.concatenate([h, l], axis=0), high[s], 1, 0, None)
        products[s] = both[:K] + both[K:] + dot(h, low[s], 1, 0, None)
        return carry

    lax.fori_loop(0, SLOTS, backward, 0, unroll=4)

    def pick(wanted, index_ref):
        total = jnp.zeros((K, BS), F32)
        for s in range(SLOTS):
            total = total + jnp.where(index_ref[0, 0, s] == wanted, 1.0, 0.0) * products[s]
        return total

    def fill_plane(plane):
        def fill(place, carry):
            pb[plane, place] = pick(lax.rem(z + offset_of(place), NZ) * NX + plane, cols_ref)
            return carry

        lax.fori_loop(0, NZ, fill, 0)

    for d in X_ORDER:
        plane = lax.rem(x + d, NX)
        fill_plane(plane)
        for h, (a, b) in enumerate(SCATTER_GROUPS):
            send_one(("sx", d, h), pb.at[plane, a:b], rbx.at[d - 1, a:b], x_peers[d - 1])

    def scatter_z(h):
        a, b = SCATTER_GROUPS[h]
        for d in X_ORDER:
            arrived(("sx", d, h), rbx.at[d - 1, a:b])
        for p in range(a, b):
            total = pb[x, p]
            for d in range(1, NX):
                total = total + rbx[d - 1, p]
            pb[x, p] = total
        for d, device in zip(z_order, z_peers):
            if a <= PLACE[d] < b:
                send("sz", pb.at[x, PLACE[d]], rbz.at[PLACE[NZ - d]], device)

    ar_next(EARLY, 1)
    fill_plane(x)

    for g, (a, b) in enumerate(GATHER_GROUPS):
        for d in X_ORDER:
            arrived(("gx", d, g), xr.at[lax.rem(x + NX - d, NX), a:b])

    def column_rows(s):
        block = cols_ref[0, 0, s]
        return xr[lax.rem(block, NX), place_of(lax.rem(lax.div(block, NX) - z + NZ, NZ))]

    def crossing(s, total):
        return total + products[s] * column_rows(s)

    cross = lax.fori_loop(0, SLOTS, crossing, jnp.zeros((K, BS), F32), unroll=4)
    cross = 2.0 * jnp.sum(cross, axis=1, keepdims=True)
    lanes = lax.broadcasted_iota(jnp.int32, (8, 128), 1)
    ar_send(CROSS, 0, jnp.where(lanes < 64, cross[:8], cross[8:]))

    def forward(s, carry):
        alive = jnp.where(s < live, 1.0, 0.0)
        h, l = split(column_rows(s) * alive)
        both = dot(jnp.concatenate([h, l], axis=0), high[s], 1, 1, None)
        products[s] = both[:K] + both[K:] + dot(h, low[s], 1, 1, None)
        return carry

    lax.fori_loop(0, SLOTS // 2, forward, 0, unroll=4)
    ar_next(CROSS, 0)
    lax.fori_loop(SLOTS // 2, SLOTS, forward, 0, unroll=4)

    def fill_core(half):
        def fill(yy, carry):
            pf[half, yy] = pick(yy * NC + half, rows_ref)
            return carry

        lax.fori_loop(0, NY, fill, 0)

    fill_core(1 - core)
    send_one("sc", pf.at[1 - core], rfc, other_core)
    ar_next(EARLY, 2)
    fill_core(core)
    ar_next(CROSS, 1)
    scatter_z(0)
    arrived("sc", rfc)

    def sum_c(yy, carry):
        pf[core, yy] = pf[core, yy] + rfc[yy]
        return carry

    lax.fori_loop(0, NY, sum_c, 0)
    for index, device in y_peers:
        send("sy", pf.at[core, index], rfy.at[y], device)
    drains.append(("sy", pf.at[0, 0 : NY - 1]))
    scatter_z(1)
    drains.append(("sz", rbz.at[0 : NZ - 1]))

    total_rows = BS * NZ * NX * NY * NC
    packed = ar_sum(EARLY, 3) / total_rows
    gram = jnp.concatenate([packed[:, 32 * i : 32 * i + 32] for i in range(4)], axis=0)
    squares = jnp.sum(gram[:K, :K] * identity(K), axis=1, keepdims=True)
    inverse = inverse_factor(gram[:K, :K], K)
    basis = dot(inverse, states)
    project = dot(gram[K:, :K], inverse, 1, 1)
    rest = directions - dot(project, basis)
    gram_rest = gram[K:, K:] - dot(project, project, 1, 1)
    loads[6].wait()
    rotation = rotation_ref[...]
    kept = dot(rotation[:, :K], basis)

    ar_next(CROSS, 2)
    arrived("sy", rfy.at[0 : NY - 1])
    applied = pf[core, y]
    for d in range(1, NY):
        applied = applied + rfy[lax.rem(y + d, NY)]
    arrived("sz", rbz.at[0 : NZ - 1])
    applied = applied + pb[x, 0]
    for place in range(1, NZ):
        applied = applied + rbz[place]
    crossed = ar_sum(CROSS, 3)
    quotient = jnp.concatenate([crossed[:, 0:1], crossed[:, 64:65]], axis=0) / (squares * total_rows)
    residual = applied - quotient * states

    left_side = jnp.concatenate([residual, rest], axis=0)
    right_side = jnp.concatenate([basis, residual, rest], axis=0)
    local = dot(left_side, right_side, 1, 1)
    wide = jnp.concatenate([local[:K], local[K:, K : 2 * K]], axis=1)
    ar_send(LATE, 0, jnp.concatenate([wide[:8], wide[8:]], axis=1))
    quotient_ref[...] = jnp.sum(identity(K) * quotient, axis=0, keepdims=True)
    ar_next(LATE, 0)
    ar_next(LATE, 1)
    ar_next(LATE, 2)
    packed = ar_sum(LATE, 3) / total_rows
    wide = jnp.concatenate([packed[:, :64], packed[:, 64:]], axis=0)
    lower = wide[:, :K]
    gram_residual = wide[:, K : 2 * K] - dot(lower, lower, 1, 1)
    top = jnp.concatenate([gram_residual, wide[:, 2 * K : 3 * K]], axis=1)
    bottom = jnp.concatenate([wide[:, 3 * K :], gram_rest], axis=1)
    inverse = inverse_factor(jnp.concatenate([top, bottom], axis=0), 2 * K)
    mixing = dot(rotation[:, K:], inverse)
    mixing = jnp.concatenate([-dot(mixing[:, :K], lower), mixing], axis=1)
    fresh = dot(mixing, right_side)
    new_direction_ref[0] = fresh
    new_states_ref[0] = kept + new_direction_ref[0]

    for name, like in drains:
        pltpu.make_async_copy(like, like, send_sem.at[stage_of(name)]).wait()


def finish(states_hbm, direction_hbm, quotient_hbm, new_states_ref, new_direction_ref, quotient_ref, sem):
    copies = [
        pltpu.make_async_copy(states_hbm, new_states_ref, sem.at[0]),
        pltpu.make_async_copy(direction_hbm, new_direction_ref, sem.at[1]),
        pltpu.make_async_copy(quotient_hbm, quotient_ref, sem.at[2]),
    ]
    for copy in copies:
        copy.start()
    for copy in copies:
        copy.wait()


def body(states, direction, blocks, counts, block_rows, block_cols, rotation):
    vmem = pl.BlockSpec(memory_space=pltpu.VMEM)
    hbm = pl.BlockSpec(memory_space=pltpu.HBM)
    outs = (
        jax.ShapeDtypeStruct((1, K, BS), F32),
        jax.ShapeDtypeStruct((1, K, BS), F32),
        jax.ShapeDtypeStruct((1, K), F32),
    )
    results = pl.pallas_call(
        kernel,
        out_shape=outs,
        in_specs=[hbm] * 7,
        out_specs=(vmem, vmem, vmem),
        scratch_shapes=[
            pltpu.VMEM((SLOTS, BS, BS), F32),
            pltpu.VMEM((SLOTS, BS, BS), BF16),
            pltpu.VMEM((SLOTS, BS, BS), BF16),
            pltpu.VMEM((NX, NZ, K, BS), F32),
            pltpu.VMEM((NC, NY, K, BS), F32),
            pltpu.VMEM((SLOTS, K, BS), F32),
            pltpu.VMEM((NX, NZ, K, BS), F32),
            pltpu.VMEM((NC, NY, K, BS), F32),
            pltpu.VMEM((NX - 1, NZ, K, BS), F32),
            pltpu.VMEM((NZ, K, BS), F32),
            pltpu.VMEM((NY, K, BS), F32),
            pltpu.VMEM((NY, K, BS), F32),
            pltpu.VMEM((K, BS), F32),
            pltpu.VMEM((3, NC, 8, 128), F32),
            pltpu.VMEM((3, NX, 8, 128), F32),
            pltpu.VMEM((3, NY, 8, 128), F32),
            pltpu.VMEM((3, NZ, 8, 128), F32),
            pltpu.SMEM((1, 1), jnp.int32),
            pltpu.SMEM((1, 1, SLOTS), jnp.int32),
            pltpu.SMEM((1, 1, SLOTS), jnp.int32),
            pltpu.VMEM((K, NSUB), F32),
            pltpu.SemaphoreType.DMA((7,)),
            pltpu.SemaphoreType.DMA((SLOTS,)),
            pltpu.SemaphoreType.DMA((STAGES,)),
            pltpu.SemaphoreType.DMA((STAGES,)),
        ],
        compiler_params=pltpu.CompilerParams(
            collective_id=0, has_side_effects=True, vmem_limit_bytes=60 * 1024 * 1024
        ),
    )(states, direction, blocks, counts, block_rows, block_cols, rotation.T)
    new_states, new_direction, quotient = pl.pallas_call(
        finish,
        out_shape=outs,
        in_specs=[hbm] * 3,
        out_specs=(hbm,) * 3,
        scratch_shapes=[pltpu.SemaphoreType.DMA((3,))],
        compiler_params=pltpu.CompilerParams(vmem_limit_bytes=60 * 1024 * 1024),
    )(*results)
    return new_states, new_direction, quotient.reshape(K)


def solution(mesh):
    return jax.shard_map(
        body,
        mesh=mesh,
        in_specs=(
            P(("row", "col"), None, None),
            P(("row", "col"), None, None),
            P("row", "col", None, None, None),
            P("row", "col"),
            P("row", "col", None),
            P("row", "col", None),
            P(),
        ),
        out_specs=(P(("row", "col"), None, None), P(("row", "col"), None, None), P()),
        check_vma=False,
    )
```

time: 68.7 us -> 62.8 us (0.914)
  local copies, waits for them, and re-layouts: 3.82 us -> 0 us
  Pallas kernels: 63.3 us -> 61.3 us
    unnamed x3 -> x0, local copies, waits for them, and re-layouts: 3.82 us -> none
    pallas_call x1 -> x2, Pallas kernels: 63.3 us -> 61.3 us  [the longest x1 59.2 us: body(): pl.pallas_call(kernel, out_shape=outs, in_specs=[hbm] * 7, out_specs=(vme...]
where the time goes in v2:
time: 62.8 us; the launch traced here: 62.6 us
  Pallas kernels  61.3 us (98%)
  between operations  1.29 us (2%)
    pallas_call x1, Pallas kernels, body(): pl.pallas_call(kernel, out_shape=outs, in_specs=[hbm] * 7, out_specs=(vme...  59.2 us
    pallas_call x1, Pallas kernels, body(): pl.pallas_call(finish, out_shape=outs, in_specs=[hbm] * 3, out_specs=(hbm...  2.14 us

profile of v2, /device:TPU:1, one launch (start us, length us, event | category | flops | bytes accessed | tf_op | source)
XLA Modules:
  0.0 62.6 jit_solution(2614130431135831723)
XLA Ops:
  1.3 59.2 %shard_map.94 = (f32[1,16,256]{2,1,0:T(8,128)}, f32[1,16,256]{2,1,0:T(8,128)}, f32[1,16]{1,0:T(1,128)}) custom-call(f32[1,16,256]{2,1,0:T(8,128)} %states_hbm.1, f32[1,16,256]{2,1,0:T(8,128)} %direction_hbm.1, f32[1,1,16,256,256]{4,3,2,1,0:T(8,128)} %blocks_hbm.1, s32[1,1]{1,0:T(1,128)S(6)} %copy.10.count_hbm, s32[1,1,16]{2,1,0:T(1,128)} %rows_hbm.1, ...), custom_call_target="tpu_custom_call" | custom-call | tf_op jit(solution)/shard_map/pallas_call | solution.py:365
  60.5 2.1 %shard_map.95 = (f32[1,16,256]{2,1,0:T(8,128)}, f32[1,16,256]{2,1,0:T(8,128)}, f32[1,16]{1,0:T(1,128)}) custom-call(f32[1,16,256]{2,1,0:T(8,128)} %get-tuple-element.9.states_hbm, f32[1,16,256]{2,1,0:T(8,128)} %get-tuple-element.10.direction_hbm, f32[1,16]{1,0:T(1,128)} %get-tuple-element.11.quotient_hbm), custom_call_target="tpu_custom_call" | custom-call | tf_op jit(solution)/shard_map/pallas_call | solution.py:401

commit v3 on v2

--- a/solution.py
+++ b/solution.py
@@ -208,17 +208,17 @@
             total = total + jnp.where(index_ref[0, 0, s] == wanted, 1.0, 0.0) * products[s]
         return total
 
-    def fill_plane(plane):
+    def fill_plane(plane, first, end):
         def fill(place, carry):
             pb[plane, place] = pick(lax.rem(z + offset_of(place), NZ) * NX + plane, cols_ref)
             return carry
 
-        lax.fori_loop(0, NZ, fill, 0)
-
-    for d in X_ORDER:
-        plane = lax.rem(x + d, NX)
-        fill_plane(plane)
-        for h, (a, b) in enumerate(SCATTER_GROUPS):
+        lax.fori_loop(first, end, fill, 0)
+
+    for h, (a, b) in enumerate(SCATTER_GROUPS):
+        for d in X_ORDER:
+            plane = lax.rem(x + d, NX)
+            fill_plane(plane, a, b)
             send_one(("sx", d, h), pb.at[plane, a:b], rbx.at[d - 1, a:b], x_peers[d - 1])
 
     def scatter_z(h):
@@ -235,7 +235,7 @@
                 send("sz", pb.at[x, PLACE[d]], rbz.at[PLACE[NZ - d]], device)
 
     ar_next(EARLY, 1)
-    fill_plane(x)
+    fill_plane(x, 0, NZ)
 
     for g, (a, b) in enumerate(GATHER_GROUPS):
         for d in X_ORDER:
@@ -275,7 +275,6 @@
     send_one("sc", pf.at[1 - core], rfc, other_core)
     ar_next(EARLY, 2)
     fill_core(core)
-    ar_next(CROSS, 1)
     scatter_z(0)
     arrived("sc", rfc)
 
@@ -287,7 +286,9 @@
     for index, device in y_peers:
         send("sy", pf.at[core, index], rfy.at[y], device)
     drains.append(("sy", pf.at[0, 0 : NY - 1]))
-    scatter_z(1)
+    ar_next(CROSS, 1)
+    for h in range(1, len(SCATTER_GROUPS)):
+        scatter_z(h)
     drains.append(("sz", rbz.at[0 : NZ - 1]))
 
     total_rows = BS * NZ * NX * NY * NC
@@ -323,6 +324,13 @@
     ar_send(LATE, 0, jnp.concatenate([wide[:8], wide[8:]], axis=1))
     quotient_ref[...] = jnp.sum(identity(K) * quotient, axis=0, keepdims=True)
     ar_next(LATE, 0)
+
+    def drain():
+        for name, like in drains:
+            pltpu.make_async_copy(like, like, send_sem.at[stage_of(name)]).wait()
+        drains.clear()
+
+    drain()
     ar_next(LATE, 1)
     ar_next(LATE, 2)
     packed = ar_sum(LATE, 3) / total_rows
@@ -333,13 +341,11 @@
     bottom = jnp.concatenate([wide[:, 3 * K :], gram_rest], axis=1)
     inverse = inverse_factor(jnp.concatenate([top, bottom], axis=0), 2 * K)
     mixing = dot(rotation[:, K:], inverse)
-    mixing = jnp.concatenate([-dot(mixing[:, :K], lower), mixing], axis=1)
-    fresh = dot(mixing, right_side)
+    fresh = dot(mixing, jnp.concatenate([residual - dot(lower, basis), rest], axis=0))
     new_direction_ref[0] = fresh
     new_states_ref[0] = kept + new_direction_ref[0]
 
-    for name, like in drains:
-        pltpu.make_async_copy(like, like, send_sem.at[stage_of(name)]).wait()
+    drain()
 
 
 def finish(states_hbm, direction_hbm, quotient_hbm, new_states_ref, new_direction_ref, quotient_ref, sem):

time: 62.8 us -> 62.6 us (level)
  no operation moved by 1% of the time
where the time goes in v3:
time: 62.6 us; the launch traced here: 62.3 us
  Pallas kernels  61 us (97%)
  between operations  1.29 us (2%)
    pallas_call x1, Pallas kernels, body(): pl.pallas_call(kernel, out_shape=outs, in_specs=[hbm] * 7, out_specs=(vme...  58.9 us
    pallas_call x1, Pallas kernels, body(): pl.pallas_call(finish, out_shape=outs, in_specs=[hbm] * 3, out_specs=(hbm...  2.14 us

profile of v3, /device:TPU:1, one launch (start us, length us, event | category | flops | bytes accessed | tf_op | source)
XLA Modules:
  0.0 62.3 jit_solution(7752770753932213561)
XLA Ops:
  1.3 58.9 %shard_map.94 = (f32[1,16,256]{2,1,0:T(8,128)}, f32[1,16,256]{2,1,0:T(8,128)}, f32[1,16]{1,0:T(1,128)}) custom-call(f32[1,16,256]{2,1,0:T(8,128)} %states_hbm.1, f32[1,16,256]{2,1,0:T(8,128)} %direction_hbm.1, f32[1,1,16,256,256]{4,3,2,1,0:T(8,128)} %blocks_hbm.1, s32[1,1]{1,0:T(1,128)S(6)} %copy.10.count_hbm, s32[1,1,16]{2,1,0:T(1,128)} %rows_hbm.1, ...), custom_call_target="tpu_custom_call" | custom-call | tf_op jit(solution)/shard_map/pallas_call | solution.py:371
  60.1 2.1 %shard_map.95 = (f32[1,16,256]{2,1,0:T(8,128)}, f32[1,16,256]{2,1,0:T(8,128)}, f32[1,16]{1,0:T(1,128)}) custom-call(f32[1,16,256]{2,1,0:T(8,128)} %get-tuple-element.9.states_hbm, f32[1,16,256]{2,1,0:T(8,128)} %get-tuple-element.10.direction_hbm, f32[1,16]{1,0:T(1,128)} %get-tuple-element.11.quotient_hbm), custom_call_target="tpu_custom_call" | custom-call | tf_op jit(solution)/shard_map/pallas_call | solution.py:407
